TPU v7x, 32 devices: a whole 2x2x4 slice. The times are simulated.
32 devices in a mesh: parts: 2 (over y), blk: 4 (over z), grp: 4 (over x, core).
Axes of the slice: x: 2, y: 2, z: 4, core: 2. Of those that a mesh axis runs over, the one named last changes fastest.
Arguments:
- node_feats: bfloat16 [16384, 256], P(('parts', 'blk', 'grp')), parts along dimension 0, may hold values from -6 to 6
- mean_feats: bfloat16 [16384, 256], P(('parts', 'blk', 'grp')), parts along dimension 0, may hold values from -6 to 6
- cotangent: bfloat16 [16384, 256], P(('parts', 'blk', 'grp')), parts along dimension 0, may hold values from -6 to 6
- w_self: bfloat16 [256, 256], replicated, may hold values from -0.375 to 0.375
- w_neigh: bfloat16 [256, 256], replicated, may hold values from -0.375 to 0.375
- degree: int32 [16384], P(('parts', 'blk', 'grp')), parts along dimension 0, may hold values from 1 to 32
- adjacency: bfloat16 [8, 4, 4, 6, 128, 128], P(('parts', 'blk'), 'grp'), parts along dimension 0, may hold values from 0 to 1, as said below
- dst_tiles: int32 [8, 4, 4, 6], P(('parts', 'blk'), 'grp'), parts along dimension 0, may hold values from 0 to 15
- src_tiles: int32 [8, 4, 4, 6], P(('parts', 'blk'), 'grp'), parts along dimension 0, may hold values from 0 to 3
- tile_counts: int32 [8, 4, 4], P(('parts', 'blk'), 'grp'), parts along dimension 0, may hold values from 1 to 6, as said below
Outputs:
- grad_input: bfloat16 [16384, 256], P(('parts', 'blk', 'grp')), parts along dimension 0
- grad_self: float32 [512, 256], P('parts'), parts along dimension 0
- grad_neigh: float32 [512, 256], P('parts'), parts along dimension 0
There are 2 independent parts, one for each index of `parts`. A program takes and returns all parts, laid end to end along the dimension named above; an argument that names none is the same for every part. Nothing has to cross between parts.
Inputs may be any that keep to these rules, and one draw needn't show every extreme that they name: `tile_counts`: every holder has at least one live slot for every source row group; some holder fills all 6 slots for some source row group in every draw. `adjacency`: entries are 0 or 1.
All inputs are finite; a program needn't handle non-finite values.
Results may differ from a plain program's by a relative error of at most 0.0046.
Values may be sent and summed in bfloat16 or wider, within the bound.
A program may use at most 128 MiB of HBM per device.

v0:
```python
import jax
import jax.numpy as jnp
from jax import lax
from jax.sharding import PartitionSpec as P


def on_device(
    node_feats,
    mean_feats,
    cotangent,
    w_self,
    w_neigh,
    degree,
    adjacency,
    dst_tiles,
    src_tiles,
    tile_counts,
):
    rows_here, width = cotangent.shape
    tile = adjacency.shape[-1]
    slot_count = adjacency.shape[3]
    dev_tiles = rows_here // tile
    nblk = lax.axis_size("blk")
    group_cot, group_deg = (
        lax.all_gather(cotangent, "grp", axis=0, tiled=True),
        lax.all_gather(degree.astype(jnp.bfloat16), "grp", axis=0, tiled=True),
    )
    scaled = group_cot.astype(jnp.float32) / group_deg.astype(jnp.float32)[:, None]
    scaled_blocks = scaled.reshape(group_cot.shape[0] // tile, tile, width)
    my_tiles = adjacency[0, 0]
    my_dst = dst_tiles[0, 0]
    my_src = src_tiles[0, 0]
    my_counts = tile_counts[0, 0]
    slot_ids = jnp.arange(slot_count, dtype=jnp.int32)
    tile_ids = jnp.arange(dev_tiles, dtype=jnp.int32)

    def contribute(target, source_blocks):
        tiles_now = lax.dynamic_index_in_dim(my_tiles, target, 0, keepdims=False)
        dst_now = lax.dynamic_index_in_dim(my_dst, target, 0, keepdims=False)
        src_now = lax.dynamic_index_in_dim(my_src, target, 0, keepdims=False)
        count_now = lax.dynamic_index_in_dim(my_counts, target, 0, keepdims=False)
        rows = jnp.take(source_blocks, dst_now, axis=0)
        parts = jnp.einsum(
            "tij,tif->tjf", tiles_now.astype(jnp.float32), rows, precision=lax.Precision.HIGHEST
        )
        live = (slot_ids < count_now).astype(jnp.float32)
        placing = (src_now[None, :] == tile_ids[:, None]).astype(jnp.float32) * live[None, :]
        added = jnp.einsum("rt,tjf->rjf", placing, parts, precision=lax.Precision.HIGHEST)
        return added.reshape(rows_here, source_blocks.shape[-1])

    targets = jnp.arange(nblk, dtype=jnp.int32)
    outgoing = jax.vmap(lambda target: contribute(target, scaled_blocks))(targets)
    incoming = lax.all_to_all(outgoing, "blk", split_axis=0, concat_axis=0, tiled=True)
    pulled = jnp.sum(incoming, axis=0)
    pulled_b = pulled.astype(jnp.bfloat16)
    own_term = lax.dot_general(
        cotangent, w_self, (((1,), (1,)), ((), ())), preferred_element_type=jnp.float32
    )
    neigh_term = lax.dot_general(
        pulled_b, w_neigh, (((1,), (1,)), ((), ())), preferred_element_type=jnp.float32
    )
    grad_input = (own_term + neigh_term).astype(jnp.bfloat16)
    self_part = lax.dot_general(
        node_feats, cotangent, (((0,), (0,)), ((), ())), preferred_element_type=jnp.float32
    )
    neigh_part = lax.dot_general(
        mean_feats, cotangent, (((0,), (0,)), ((), ())), preferred_element_type=jnp.float32
    )
    self_total, neigh_total = lax.psum((self_part, neigh_part), ("blk", "grp"))
    factor = (rows_here * nblk * lax.axis_size("grp")) ** (-0.5)
    return (grad_input, self_total * factor, neigh_total * factor)


def solution(mesh):
    placed = (
        P(("parts", "blk", "grp"), None),
        P(("parts", "blk", "grp"), None),
        P(("parts", "blk", "grp"), None),
        P(),
        P(),
        P(("parts", "blk", "grp")),
        P(("parts", "blk"), "grp", None, None, None, None),
        P(("parts", "blk"), "grp", None, None),
        P(("parts", "blk"), "grp", None, None),
        P(("parts", "blk"), "grp", None),
    )
    return jax.shard_map(
        on_device,
        mesh=mesh,
        in_specs=placed,
        out_specs=(P(("parts", "blk", "grp"), None), P("parts", None), P("parts", None)),
        check_vma=False,
    )
```

profile of v0, /device:TPU:0, one launch (start us, length us, event | category | flops | bytes accessed | tf_op | source)
XLA Modules:
  0.0 178.2 jit_solution(8026633809916471526)
XLA Ops:
  8.0 0.0 copy-start
  8.0 0.0 all-gather.3.cloned.1.call-start
  8.1 0.7 all-gather.3.cloned.1.call-update
  8.8 1.3 gather_fusion.3
  10.0 0.1 reshape.99
  10.1 0.7 convert_element_type.26
  10.8 6.1 %all-gather = bf16[4,1,512]{2,1,0:T(2,128)(2,1)S(1)} all-gather(bf16[1,1,512]{2,1,0:T(2,128)(2,1)S(1)} %reshape.111), channel_id=1, replica_groups=mesh['parts'=2,'blk'=4,'grp'=4] {'grp'}, dimensions={0}, use_global_device_ids=true | all-gather | bytes 5120 | tf_op jit(solution)/shard_map/all_gather | solution.py:26
  16.9 1.3 gather_fusion
  18.2 0.0 copy-done
  18.2 1.5 gather_fusion.2
  19.8 1.3 gather_fusion.1
  21.1 0.1 fusion.13
  21.1 8.7 %all-gather.3.cloned.1.call-done = bf16[2048,256]{1,0:T(8,128)(2,1)} async-done(((bf16[512,256]{1,0:T(8,128)(2,1)}), bf16[2048,256]{1,0:T(8,128)(2,1)}) %all-gather.3.cloned.1.call-update) | async-done | bytes 1048592 | tf_op jit(solution)/shard_map/all_gather | solution.py:25
  29.9 1.6 convert_divide_fusion
  31.4 2.4 %gather_fusion.4 = f32[24,128,256]{2,1,0:T(8,128)} fusion(f32[16,128,256]{2,1,0:T(8,128)S(1)} %bitcast.30, s32[1024]{0:T(1024)S(1)} %pad_clamp_fusion), kind=kCustom, calls=%fused_computation.4 | custom fusion | bytes 6291552 | tf_op jit(solution)/shard_map/vmap(jit(_take))/gather | solution.py:42
  33.8 4.3 %fusion.2 = f32[4,6,128,256]{3,2,1,0:T(8,128)S(1)} fusion(bf16[4,6,128,128]{3,2,1,0:T(8,128)(2,1)} %gather_fusion.2, f32[4,6,128,256]{3,2,1,0:T(8,128)} %bitcast.31, pred[4,6]{1,0:T(4,128)(4,1)S(1)} %compare_and_fusion), kind=kOutput, calls=%fused_computation.7 | convolution fusion | flops 1208745984 | bytes 7077912 | tf_op jit(solution)/shard_map/vmap(tij,tif->tjf)/dot_general | solution.py:43
  38.1 5.2 %fusion = f32[4,4,128,256]{3,1,2,0:T(4,128)S(1)} fusion(f32[4,6,128,256]{3,2,1,0:T(8,128)S(1)} %fusion.2, s32[4,6]{1,0:T(4,128)S(1)} %gather_fusion, f32[4,6]{1,0:T(4,128)S(1)} %fusion.13), kind=kOutput, calls=%fused_computation.5 | convolution fusion | flops 37748928 | bytes 5243072 | tf_op jit(solution)/shard_map/vmap(rt,tjf->rjf)/dot_general | solution.py:48
  43.3 1.7 copy.16
  45.0 0.0 copy-start.1
  45.0 0.0 copy-start.3
  45.0 0.0 copy-start.4
  45.0 4.7 %all-to-all-start = ((f32[4,512,256]{2,1,0:T(8,128)}), f32[4,512,256]{2,1,0:T(8,128)S(1)}, u32[]{:S(2)}, u32[]{:S(2)}) async-start(f32[4,512,256]{2,1,0:T(8,128)} %bitcast.32), calls=%async_computation | async-start | bytes 4194304 | tf_op jit(solution)/shard_map/all_to_all | solution.py:53
  49.8 0.0 all-reduce.3.cloned.1.call-start
  49.8 0.0 copy-done.1
  49.8 0.0 copy-done.3
  49.8 1.0 fusion.17
  50.7 1.9 %fusion.18 = f32[256,256]{1,0:T(8,128)} fusion(bf16[512,256]{1,0:T(8,128)(2,1)} %param.11, bf16[512,256]{1,0:T(8,128)(2,1)S(1)} %copy-done.1), kind=kOutput, calls=%fused_computation.35 | convolution fusion | flops 67108864 | bytes 786432 | tf_op jit(solution)/shard_map/dot_general | solution.py:66
  52.7 0.0 all-reduce.3.cloned.1.call-update
  52.7 0.0 copy-done.4
  52.7 1.1 fusion.16
  53.8 0.0 copy-start.2
  53.8 0.0 copy-start.5
  53.8 112.4 %all-reduce.3.cloned.1.call-done = (f32[256,256]{1,0:T(8,128)}, f32[256,256]{1,0:T(8,128)}) async-done(((f32[256,256]{1,0:T(8,128)}, f32[256,256]{1,0:T(8,128)}), (f32[256,256]{1,0:T(8,128)}, f32[256,256]{1,0:T(8,128)})) %all-reduce.3.cloned.1.call-update) | async-done | bytes 524304 | tf_op jit(solution)/shard_map/psum | solution.py:69
  166.1 1.9 %broadcast_multiply_fusion = (f32[256,256]{1,0:T(8,128)}, f32[256,256]{1,0:T(8,128)}) fusion(f32[256,256]{1,0:T(8,128)} %get-tuple-element.4, f32[256,256]{1,0:T(8,128)} %get-tuple-element.3), kind=kLoop, calls=%fused_computation.15 | loop fusion | flops 131072 | bytes 1048576 | tf_op jit(solution)/shard_map/mul | solution.py:71
  168.0 0.0 all-to-all-done
  168.0 0.9 reduce_sum.9
  168.9 0.0 copy-done.2
  168.9 0.0 copy-done.5
  168.9 1.9 %fusion.6 = bf16[512,256]{1,0:T(8,128)(2,1)} fusion(f32[512,256]{1,0:T(8,128)S(1)} %copy-done.2, bf16[256,256]{1,0:T(8,128)(2,1)S(1)} %copy-done.5, bf16[512,256]{1,0:T(8,128)(2,1)} %reduce_sum.9), kind=kOutput, calls=%fused_computation.13 | convolution fusion | flops 67371008 | bytes 1179648 | tf_op jit(solution)/shard_map/dot_general | solution.py:59
  (9 shorter events, 0.1 us)
Async XLA Ops:
  8.0 10.2 %copy-start = (bf16[1,1,4,6,128,128]{5,4,3,2,1,0:T(8,128)(2,1)S(1)}, bf16[1,1,4,6,128,128]{5,4,3,2,1,0:T(8,128)(2,1)}, u32[]{:S(2)}) copy-start(bf16[1,1,4,6,128,128]{5,4,3,2,1,0:T(8,128)(2,1)} %param.16) | copy-start | bytes 2359300
  8.0 21.8 %all-gather.3.cloned.1.call-start = ((), (), s32[]{:S(2)}) async-start(), calls=%async_computation.1 | async-start | bytes 1310720 | tf_op jit(solution)/shard_map/all_gather | solution.py:25
  45.0 4.7 %copy-start.1 = (bf16[512,256]{1,0:T(8,128)(2,1)S(1)}, bf16[512,256]{1,0:T(8,128)(2,1)}, u32[]{:S(2)}) copy-start(bf16[512,256]{1,0:T(8,128)(2,1)} %param.12) | copy-start | bytes 786436
  45.0 4.7 %copy-start.3 = (bf16[512,256]{1,0:T(8,128)(2,1)S(1)}, bf16[512,256]{1,0:T(8,128)(2,1)}, u32[]{:S(2)}) copy-start(bf16[512,256]{1,0:T(8,128)(2,1)} %param.10) | copy-start | bytes 786436
  45.0 7.7 %copy-start.4 = (bf16[256,256]{1,0:T(8,128)(2,1)S(1)}, bf16[256,256]{1,0:T(8,128)(2,1)}, u32[]{:S(2)}) copy-start(bf16[256,256]{1,0:T(8,128)(2,1)} %param.13) | copy-start | bytes 393220
  45.0 123.0 %all-to-all-start = ((f32[4,512,256]{2,1,0:T(8,128)}), f32[4,512,256]{2,1,0:T(8,128)S(1)}, u32[]{:S(2)}, u32[]{:S(2)}) async-start(f32[4,512,256]{2,1,0:T(8,128)} %bitcast.32), calls=%async_computation | async-start | bytes 4194304 | tf_op jit(solution)/shard_map/all_to_all | solution.py:53
  49.8 116.4 %all-reduce.3.cloned.1.call-start = ((), (), s32[]{:S(2)}) async-start(), calls=%async_computation.2 | async-start | bytes 1048576 | tf_op jit(solution)/shard_map/psum | solution.py:69
  53.8 115.1 %copy-start.2 = (f32[512,256]{1,0:T(8,128)S(1)}, f32[512,256]{1,0:T(8,128)}, u32[]{:S(2)}) copy-start(f32[512,256]{1,0:T(8,128)} %fusion.16) | copy-start | bytes 1572868
  53.8 115.1 %copy-start.5 = (bf16[256,256]{1,0:T(8,128)(2,1)S(1)}, bf16[256,256]{1,0:T(8,128)(2,1)}, u32[]{:S(2)}) copy-start(bf16[256,256]{1,0:T(8,128)(2,1)} %param.14) | copy-start | bytes 393220
Sparse Core Ops, SparseCore 0:
  10.4 19.4 all-gather.2
Sparse Core Ops, SparseCore 1:
  54.2 111.8 all-reduce.2
where the time goes:
time: 179 us; the launch traced here: 178 us
  waiting for transfers between devices  122 us (68%)
  between operations  15.6 us (9%)
  matrix products  15.4 us (9%)
  local copies, waits for them, and re-layouts  9.56 us (5%)
  blocking collectives  6.1 us (3%)
  other arithmetic  5.11 us (3%)
  starting transfers between devices  4.77 us (3%)
    psum x1, waiting for transfers between devices, on_device(): self_total, neigh_total = lax.psum((self_part, neigh_part), ('blk', 'grp'))  112 us
    all_gather x1, waiting for transfers between devices, on_device(): lax.all_gather(cotangent, 'grp', axis=0, tiled=True)  8.73 us
    all_gather x1, blocking collectives, on_device(): lax.all_gather(degree.astype(jnp.bfloat16), 'grp', axis=0, tiled=True)  6.1 us
    dot_general x1, matrix products, contribute(): jnp.einsum('rt,tjf->rjf', placing, parts, precision=lax.Precision.HIGHEST)  5.18 us
    all_to_all x1, starting transfers between devices, on_device(): lax.all_to_all(outgoing, 'blk', split_axis=0, concat_axis=0, tiled=True)  4.73 us
    dot_general x1, matrix products, contribute(): jnp.einsum('tij,tif->tjf', tiles_now.astype(jnp.float32), rows, precision...  4.31 us
  transfers between devices with their start and end apart: 3, of which 2 were waited for; matrix products, arithmetic and copies ran while one was open for 7% of the time, Pallas kernels for 0%

commit v1 on v0

v1 whole, which is shorter than its diff:
```python
import functools

import jax
import jax.numpy as jnp
from jax import lax
from jax.experimental import pallas as pl
from jax.experimental.pallas import tpu as pltpu
from jax.sharding import PartitionSpec as P

MESH = pl.DeviceIdType.MESH
F32, BF16 = jnp.float32, jnp.bfloat16
HALVES = 2


def kernel(
    dims,
    cot, node, mean, w_self, w_neigh, deg, adj, dst, src, cnt,
    gin, gself, gneigh,
    cot_v, node_v, mean_v, ws_v, wn_v, adj_v,
    cot_in0, cot_in1, deg_in, scaled0, scaled1, placed,
    part_out0, part_out1, part_in0, part_in1, acc0, acc1, own,
    w_acc, w_out, wz_in, wq, wg_in, zag, gag,
    load_sem, gs, gr, ds, dr, ps, pr_sem, zs, zr, qs, qr, as_, ar, bs, br,
):
    ng, nb, tile, slots, dev_tiles, rows, width, rq, pr, owners = dims
    half = width // HALVES
    g, b = lax.axis_index("grp"), lax.axis_index("blk")
    cot_in, scaled = (cot_in0, cot_in1), (scaled0, scaled1)
    part_out, part_in, acc = (part_out0, part_out1), (part_in0, part_in1), (acc0, acc1)

    loads = [
        pltpu.make_async_copy(a, v, load_sem.at[i])
        for i, (a, v) in enumerate(
            ((cot, cot_v), (node, node_v), (mean, mean_v), (adj, adj_v), (w_self, ws_v), (w_neigh, wn_v))
        )
    ]
    for c in loads:
        c.start()

    barrier = pltpu.get_barrier_semaphore()
    for d in range(1, ng):
        pl.semaphore_signal(barrier, inc=1, device_id={"grp": lax.rem(g + d, ng)}, device_id_type=MESH)
    for d in range(1, nb):
        pl.semaphore_signal(barrier, inc=1, device_id={"blk": lax.rem(b + d, nb)}, device_id_type=MESH)
    pl.semaphore_wait(barrier, ng - 1 + nb - 1)

    def deg_copy(d):
        return pltpu.make_async_remote_copy(
            src_ref=deg, dst_ref=deg_in.at[d - 1], send_sem=ds.at[d - 1], recv_sem=dr.at[d - 1],
            device_id={"grp": lax.rem(g + d, ng)}, device_id_type=MESH)

    def cot_copy(h, d):
        return pltpu.make_async_remote_copy(
            src_ref=cot.at[:, pl.ds(h * half, half)], dst_ref=cot_in[h].at[d - 1],
            send_sem=gs.at[h, d - 1], recv_sem=gr.at[h, d - 1],
            device_id={"grp": lax.rem(g + d, ng)}, device_id_type=MESH)

    for d in range(1, ng):
        deg_copy(d).start()
    for h in range(HALVES):
        for d in range(1, ng):
            cot_copy(h, d).start()

    for c in loads[:3]:
        c.wait()
    dims0 = (((0,), (0,)), ((), ()))
    for i, feats in enumerate((node_v, mean_v)):
        w = lax.dot_general(feats[...], cot_v[...], dims0, preferred_element_type=F32)
        w_acc[i * width:(i + 1) * width, :] = w
        w_out[i * width:(i + 1) * width, :] = w.astype(BF16)

    def wz_copy(d):
        to = lax.rem(b + d, nb)
        return pltpu.make_async_remote_copy(
            src_ref=w_out.at[pl.ds(pl.multiple_of(to * rq, rq), rq), :], dst_ref=wz_in.at[d - 1],
            send_sem=zs.at[d - 1], recv_sem=zr.at[d - 1],
            device_id={"blk": to}, device_id_type=MESH)

    for d in range(1, nb):
        wz_copy(d).start()

    loads[3].wait()

    def place(s, carry):
        for t in range(slots):
            turned = adj_v[0, 0, s, t].astype(F32).T
            live = t < cnt[0, 0, s]
            at = src[0, 0, s, t]
            for j in range(dev_tiles):
                keep = jnp.where(jnp.logical_and(live, at == j), 1.0, 0.0)
                placed[s, j * tile:(j + 1) * tile, t * tile:(t + 1) * tile] = (turned * keep).astype(BF16)
        return carry

    lax.fori_loop(0, nb, place, 0)

    loads[4].wait()
    loads[5].wait()
    dims1 = (((1,), (1,)), ((), ()))
    own[...] = lax.dot_general(cot_v[...], ws_v[...], dims1, preferred_element_type=F32)

    eye = lax.broadcasted_iota(jnp.int32, (tile, tile), 0) == lax.broadcasted_iota(jnp.int32, (tile, tile), 1)

    def scale(h, owner, values, degrees):
        for k in range(dev_tiles):
            line = jnp.broadcast_to(degrees[k:k + 1, :].astype(F32), (tile, tile))
            inv = 1.0 / jnp.sum(jnp.where(eye, line, 0.0), axis=1, keepdims=True)
            x = values[k * tile:(k + 1) * tile, :].astype(F32) * inv
            hi = x.astype(BF16)
            lo = (x - hi.astype(F32)).astype(BF16)
            scaled[h][owner * dev_tiles + k, :, 0:half] = hi
            scaled[h][owner * dev_tiles + k, :, half:2 * half] = lo

    def partial(h, to):
        picked = jnp.concatenate([scaled[h][dst[0, 0, to, t]] for t in range(slots)], axis=0)
        both = jnp.dot(placed[to], picked, preferred_element_type=F32)
        return both[:, :half] + both[:, half:]

    def part_copy(h, d):
        return pltpu.make_async_remote_copy(
            src_ref=part_out[h].at[d - 1], dst_ref=part_in[h].at[d - 1],
            send_sem=ps.at[h, d - 1], recv_sem=pr_sem.at[h, d - 1],
            device_id={"blk": lax.rem(b + d, nb)}, device_id_type=MESH)

    def wg_copy(d):
        to = lax.rem(g + d, ng)
        at = lax.rem(to, owners)
        return to, pltpu.make_async_remote_copy(
            src_ref=wq.at[pl.ds(pl.multiple_of(at * pr, pr), pr), :], dst_ref=wg_in.at[d - 1],
            send_sem=qs.at[d - 1], recv_sem=qr.at[d - 1],
            device_id={"grp": to}, device_id_type=MESH)

    def zag_copy(d):
        return pltpu.make_async_remote_copy(
            src_ref=zag.at[b], dst_ref=zag.at[b], send_sem=as_.at[d - 1], recv_sem=ar.at[d - 1],
            device_id={"blk": lax.rem(b + d, nb)}, device_id_type=MESH)

    def gag_copy(d):
        return pltpu.make_async_remote_copy(
            src_ref=zag, dst_ref=gag.at[d - 1], send_sem=bs.at[d - 1], recv_sem=br.at[d - 1],
            device_id={"grp": lax.rem(g + d, ng)}, device_id_type=MESH)

    for h in range(HALVES):
        scale(h, g, cot_v[:, h * half:(h + 1) * half], deg[...])
        for d in range(1, ng):
            if h == 0:
                deg_copy(d).wait_recv()
            cot_copy(h, d).wait_recv()
            scale(h, lax.rem(g - d + ng, ng), cot_in[h][d - 1], deg_in[d - 1])

        def send_part(d, carry, h=h):
            part_out[h][d - 1] = partial(h, lax.rem(b + d, nb)).astype(BF16)
            part_copy(h, d).start()
            return carry

        lax.fori_loop(1, nb, send_part, 0)
        acc[h][...] = partial(h, b)

        if h == 0:
            total = w_acc[pl.ds(pl.multiple_of(b * rq, rq), rq), :]
            for d in range(1, nb):
                wz_copy(d).wait_recv()
                total = total + wz_in[d - 1].astype(F32)
            wq[...] = total
            for d in range(1, ng):
                to, copy = wg_copy(d)
                pl.when(to < owners)(copy.start)

    factor = (rows * nb * ng) ** (-0.5)

    @pl.when(g < owners)
    def _():
        total = wq[pl.ds(pl.multiple_of(lax.rem(g, owners) * pr, pr), pr), :]
        for d in range(1, ng):
            wg_copy(d)[1].wait_recv()
            total = total + wg_in[d - 1]
        zag[b] = (total * factor).astype(BF16)
        for d in range(1, nb):
            zag_copy(d).start()
        for d in range(1, nb):
            zag_copy(d).wait_recv()
        for d in range(1, ng):
            gag_copy(d).start()

    pulled = []
    for h in range(HALVES):
        total = acc[h][...]
        for d in range(1, nb):
            part_copy(h, d).wait_recv()
            total = total + part_in[h][d - 1].astype(F32)
        pulled.append(total.astype(BF16))
    neigh = lax.dot_general(jnp.concatenate(pulled, axis=1), wn_v[...], dims1, preferred_element_type=F32)
    gin[...] = (own[...] + neigh).astype(BF16)

    def write(q, first, values):
        per = width // rq
        for out, base in ((gself, 0), (gneigh, per)):
            if q // per * per == base:
                out[pl.ds(pl.multiple_of((q - base) * rq + first, pr), pr), :] = values.astype(F32)

    @pl.when(g < owners)
    def _():
        for q in range(nb):
            write(q, lax.rem(g, owners) * pr, zag[q])

    for d in range(1, ng):
        owner = lax.rem(g - d + ng, ng)

        @pl.when(owner < owners)
        def _(d=d, owner=owner):
            gag_copy(d).wait_recv()
            for q in range(nb):
                write(q, lax.rem(owner, owners) * pr, gag[d - 1, q])

    for d in range(1, ng):
        deg_copy(d).wait_send()
        for h in range(HALVES):
            cot_copy(h, d).wait_send()
        to, copy = wg_copy(d)
        pl.when(to < owners)(copy.wait_send)
        pl.when(g < owners)(gag_copy(d).wait_send)
    for d in range(1, nb):
        wz_copy(d).wait_send()
        for h in range(HALVES):
            part_copy(h, d).wait_send()
        pl.when(g < owners)(zag_copy(d).wait_send)


def on_device(nb, ng, node_feats, mean_feats, cotangent, w_self, w_neigh, degree, adjacency, dst_tiles, src_tiles, tile_counts):
    rows, width = cotangent.shape
    tile, slots = adjacency.shape[-1], adjacency.shape[3]
    dev_tiles = rows // tile
    half = width // HALVES
    rq = 2 * width // nb
    pr = max(16, rq // ng)
    owners = rq // pr
    dims = (ng, nb, tile, slots, dev_tiles, rows, width, rq, pr, owners)
    any_spec = pl.BlockSpec(memory_space=pl.ANY)
    vmem, smem = pl.BlockSpec(memory_space=pltpu.VMEM), pl.BlockSpec(memory_space=pltpu.SMEM)
    dma = pltpu.SemaphoreType.DMA
    V = pltpu.VMEM
    return pl.pallas_call(
        functools.partial(kernel, dims),
        out_shape=(
            jax.ShapeDtypeStruct((rows, width), BF16),
            jax.ShapeDtypeStruct((width, width), F32),
            jax.ShapeDtypeStruct((width, width), F32),
        ),
        in_specs=[any_spec] * 5 + [vmem, any_spec] + [smem] * 3,
        out_specs=(vmem, vmem, vmem),
        scratch_shapes=[
            V((rows, width), BF16), V((rows, width), BF16), V((rows, width), BF16),
            V((width, width), BF16), V((width, width), BF16), V(adjacency.shape, BF16),
            V((ng - 1, rows, half), BF16), V((ng - 1, rows, half), BF16),
            V((ng - 1, dev_tiles, tile), jnp.int32),
            V((ng * dev_tiles, tile, width), BF16), V((ng * dev_tiles, tile, width), BF16),
            V((nb, rows, slots * tile), BF16),
            V((nb - 1, rows, half), BF16), V((nb - 1, rows, half), BF16),
            V((nb - 1, rows, half), BF16), V((nb - 1, rows, half), BF16),
            V((rows, half), F32), V((rows, half), F32), V((rows, width), F32),
            V((2 * width, width), F32), V((2 * width, width), BF16), V((nb - 1, rq, width), BF16),
            V((rq, width), F32), V((ng - 1, pr, width), F32),
            V((nb, pr, width), BF16), V((ng - 1, nb, pr, width), BF16),
            dma((6,)),
            dma((HALVES, ng - 1)), dma((HALVES, ng - 1)), dma((ng - 1,)), dma((ng - 1,)),
            dma((HALVES, nb - 1)), dma((HALVES, nb - 1)), dma((nb - 1,)), dma((nb - 1,)),
            dma((ng - 1,)), dma((ng - 1,)), dma((nb - 1,)), dma((nb - 1,)), dma((ng - 1,)), dma((ng - 1,)),
        ],
        compiler_params=pltpu.CompilerParams(
            collective_id=0, has_side_effects=True, vmem_limit_bytes=56 * 1024 * 1024
        ),
    )(
        cotangent, node_feats, mean_feats, w_self, w_neigh, degree.reshape(dev_tiles, tile),
        adjacency, dst_tiles, src_tiles, tile_counts,
    )


def solution(mesh):
    placed = (
        P(("parts", "blk", "grp"), None),
        P(("parts", "blk", "grp"), None),
        P(("parts", "blk", "grp"), None),
        P(),
        P(),
        P(("parts", "blk", "grp")),
        P(("parts", "blk"), "grp", None, None, None, None),
        P(("parts", "blk"), "grp", None, None),
        P(("parts", "blk"), "grp", None, None),
        P(("parts", "blk"), "grp", None),
    )
    return jax.shard_map(
        functools.partial(on_device, mesh.shape["blk"], mesh.shape["grp"]),
        mesh=mesh,
        in_specs=placed,
        out_specs=(P(("parts", "blk", "grp"), None), P("parts", None), P("parts", None)),
        check_vma=False,
    )
```

time: 179 us -> 48.1 us (0.27)
  waiting for transfers between devices: 122 us -> 0 us
  Pallas kernels: 0 us -> 43.1 us
  matrix products: 15.4 us -> 0 us
  between operations: 15.6 us -> 0.65 us
  local copies, waits for them, and re-layouts: 9.56 us -> 3.46 us
  blocking collectives: 6.1 us -> 0 us
  other arithmetic: 5.11 us -> 0 us
  starting transfers between devices: 4.77 us -> 0 us
    psum x1 -> x0, waiting for transfers between devices: 112 us -> none  [on_device(): self_total, neigh_total = lax.psum((self_part, neigh_part), ('blk', 'grp'))]
    pallas_call x0 -> x1, Pallas kernels: none -> 43.1 us  [on_device(): pl.pallas_call(functools.partial(kernel, dims), out_shape=(jax.ShapeDtype...]
    dot_general x6 -> x0, matrix products: 15.4 us -> none  [the longest x1 5.18 us: contribute(): jnp.einsum('rt,tjf->rjf', placing, parts, precision=lax.Precision.HIGHEST)]
    all_gather x1 -> x0, waiting for transfers between devices: 8.73 us -> none  [on_device(): lax.all_gather(cotangent, 'grp', axis=0, tiled=True)]
    gather x5 -> x0, local copies, waits for them, and re-layouts: 7.73 us -> none  [the longest x1 2.38 us: contribute(): rows = jnp.take(source_blocks, dst_now, axis=0)]
    all_gather x1 -> x0, blocking collectives: 6.1 us -> none  [on_device(): lax.all_gather(degree.astype(jnp.bfloat16), 'grp', axis=0, tiled=True)]
    all_to_all x1 -> x0, starting transfers between devices: 4.73 us -> none  [on_device(): lax.all_to_all(outgoing, 'blk', split_axis=0, concat_axis=0, tiled=True)]
    unnamed x13 -> x7, local copies, waits for them, and re-layouts: 0.03 us -> 3.46 us
  transfers between devices with their start and end apart: 3 -> 0, of which waited for: 2 -> 0; matrix products, arithmetic and copies ran while one was open for 7% -> 0% of each run, Pallas kernels for 0% -> 0%
where the time goes in v1:
time: 48.1 us; the launch traced here: 47.2 us
  Pallas kernels  43.1 us (90%)
  local copies, waits for them, and re-layouts  3.46 us (7%)
  between operations  0.65 us (1%)
    pallas_call x1, Pallas kernels, on_device(): pl.pallas_call(functools.partial(kernel, dims), out_shape=(jax.ShapeDtype...  43.1 us
    unnamed x7, local copies, waits for them, and re-layouts  3.46 us

profile of v1, /device:TPU:0, one launch (start us, length us, event | category | flops | bytes accessed | tf_op | source)
XLA Modules:
  0.0 47.2 jit_solution(9930820174023915849)
XLA Ops:
  0.6 43.1 %shard_map.121 = (bf16[512,256]{1,0:T(8,128)(2,1)}, f32[256,256]{1,0:T(8,128)}, f32[256,256]{1,0:T(8,128)}) custom-call(bf16[512,256]{1,0:T(8,128)(2,1)} %cot.1, bf16[512,256]{1,0:T(8,128)(2,1)} %node.1, bf16[512,256]{1,0:T(8,128)(2,1)} %mean.1, bf16[256,256]{1,0:T(8,128)(2,1)} %w_self.1, bf16[256,256]{1,0:T(8,128)(2,1)} %w_neigh.1, s32[4,128]{1,0:T(4,128)} %bitcast.1, ...), custom_call_target="tpu_custom_call" | custom-call | tf_op jit(solution)/shard_map/pallas_call | solution.py:241
  43.7 0.0 copy-start.1
  43.8 1.7 %copy.16 = bf16[512,256]{1,0:T(8,128)(2,1)} copy(bf16[512,256]{1,0:T(8,128)(2,1)} %get-tuple-element.6) | data formatting | bytes 524288
  45.5 0.0 copy-done.1
  45.5 0.0 copy-start
  45.5 0.7 %copy.17 = f32[256,256]{1,0:T(8,128)} copy(f32[256,256]{1,0:T(8,128)S(1)} %copy-done.1) | data formatting | bytes 524288
  46.2 0.3 copy-done
  46.5 0.7 %copy.18 = f32[256,256]{1,0:T(8,128)} copy(f32[256,256]{1,0:T(8,128)S(1)} %copy-done) | data formatting | bytes 524288
Async XLA Ops:
  43.7 1.7 %copy-start.1 = (f32[256,256]{1,0:T(8,128)S(1)}, f32[256,256]{1,0:T(8,128)}, u32[]{:S(2)}) copy-start(f32[256,256]{1,0:T(8,128)} %get-tuple-element.7) | copy-start | bytes 786436
  45.5 1.0 %copy-start = (f32[256,256]{1,0:T(8,128)S(1)}, f32[256,256]{1,0:T(8,128)}, u32[]{:S(2)}) copy-start(f32[256,256]{1,0:T(8,128)} %get-tuple-element.8) | copy-start | bytes 786436

commit v2 on v1

--- a/solution.py
+++ b/solution.py
@@ -14,16 +14,17 @@
 
 def kernel(
     dims,
-    cot, node, mean, w_self, w_neigh, deg, adj, dst, src, cnt,
-    gin, gself, gneigh,
-    cot_v, node_v, mean_v, ws_v, wn_v, adj_v,
+    cot, node, mean, deg, adj, dst, src, cnt,
+    pulled_b, w_sum,
+    cot_v, node_v, mean_v, adj_v,
     cot_in0, cot_in1, deg_in, scaled0, scaled1, placed,
-    part_out0, part_out1, part_in0, part_in1, acc0, acc1, own,
+    part_out0, part_out1, part_in0, part_in1, acc0, acc1, relay_in,
     w_acc, w_out, wz_in, wq, wg_in, zag, gag,
-    load_sem, gs, gr, ds, dr, ps, pr_sem, zs, zr, qs, qr, as_, ar, bs, br,
+    load_sem, gs, gr, ds, dr, ps, pr_sem, rr, zs, zr, qs, qr, as_, ar, bs, br,
 ):
     ng, nb, tile, slots, dev_tiles, rows, width, rq, pr, owners = dims
     half = width // HALVES
+    relay = nb >= 4
     g, b = lax.axis_index("grp"), lax.axis_index("blk")
     cot_in, scaled = (cot_in0, cot_in1), (scaled0, scaled1)
     part_out, part_in, acc = (part_out0, part_out1), (part_in0, part_in1), (acc0, acc1)
@@ -31,7 +32,7 @@
     loads = [
         pltpu.make_async_copy(a, v, load_sem.at[i])
         for i, (a, v) in enumerate(
-            ((cot, cot_v), (node, node_v), (mean, mean_v), (adj, adj_v), (w_self, ws_v), (w_neigh, wn_v))
+            ((cot, cot_v), (node, node_v), (mean, mean_v), (adj, adj_v))
         )
     ]
     for c in loads:
@@ -49,17 +50,34 @@
             src_ref=deg, dst_ref=deg_in.at[d - 1], send_sem=ds.at[d - 1], recv_sem=dr.at[d - 1],
             device_id={"grp": lax.rem(g + d, ng)}, device_id_type=MESH)
 
+    sib = g + 1 - 2 * lax.rem(g, 2)
+
     def cot_copy(h, d):
-        return pltpu.make_async_remote_copy(
-            src_ref=cot.at[:, pl.ds(h * half, half)], dst_ref=cot_in[h].at[d - 1],
-            send_sem=gs.at[h, d - 1], recv_sem=gr.at[h, d - 1],
-            device_id={"grp": lax.rem(g + d, ng)}, device_id_type=MESH)
+        to = sib if d == 0 else lax.rem(g + d, ng)
+        return pltpu.make_async_remote_copy(
+            src_ref=cot.at[:, pl.ds(h * half, half)], dst_ref=cot_in[h].at[g],
+            send_sem=gs.at[h, 0, d // 2], recv_sem=gr.at[h, g],
+            device_id={"grp": to}, device_id_type=MESH)
+
+    def fwd_copy(h, d):
+        owner = lax.rem(g - d + ng, ng)
+        return pltpu.make_async_remote_copy(
+            src_ref=cot_in[h].at[owner], dst_ref=cot_in[h].at[owner],
+            send_sem=gs.at[h, 1, d // 2], recv_sem=gr.at[h, owner],
+            device_id={"grp": sib}, device_id_type=MESH)
+
+    def cot_arrival(h, owner):
+        return pltpu.make_async_remote_copy(
+            src_ref=cot_in[h].at[owner], dst_ref=cot_in[h].at[owner],
+            send_sem=gs.at[h, 0, 0], recv_sem=gr.at[h, owner],
+            device_id={"grp": sib}, device_id_type=MESH)
 
     for d in range(1, ng):
         deg_copy(d).start()
     for h in range(HALVES):
-        for d in range(1, ng):
+        for d in range(2, ng, 2):
             cot_copy(h, d).start()
+        cot_copy(h, 0).start()
 
     for c in loads[:3]:
         c.wait()
@@ -93,11 +111,6 @@
 
     lax.fori_loop(0, nb, place, 0)
 
-    loads[4].wait()
-    loads[5].wait()
-    dims1 = (((1,), (1,)), ((), ()))
-    own[...] = lax.dot_general(cot_v[...], ws_v[...], dims1, preferred_element_type=F32)
-
     eye = lax.broadcasted_iota(jnp.int32, (tile, tile), 0) == lax.broadcasted_iota(jnp.int32, (tile, tile), 1)
 
     def scale(h, owner, values, degrees):
@@ -121,6 +134,12 @@
             send_sem=ps.at[h, d - 1], recv_sem=pr_sem.at[h, d - 1],
             device_id={"blk": lax.rem(b + d, nb)}, device_id_type=MESH)
 
+    def relay_copy(h, d):
+        return pltpu.make_async_remote_copy(
+            src_ref=part_out[h].at[d - 1], dst_ref=relay_in.at[h],
+            send_sem=ps.at[h, d - 1], recv_sem=rr.at[h],
+            device_id={"blk": 1 + (nb - 3) * (b // (nb - 1))}, device_id_type=MESH)
+
     def wg_copy(d):
         to = lax.rem(g + d, ng)
         at = lax.rem(to, owners)
@@ -139,20 +158,74 @@
             src_ref=zag, dst_ref=gag.at[d - 1], send_sem=bs.at[d - 1], recv_sem=br.at[d - 1],
             device_id={"grp": lax.rem(g + d, ng)}, device_id_type=MESH)
 
+    at_end = jnp.logical_or(b == 0, b == nb - 1)
+    next_to_end = jnp.logical_or(b == 1, b == nb - 2)
+    upper = b // (nb // 2)
+    factor = (rows * nb * ng) ** (-0.5)
+
     for h in range(HALVES):
         scale(h, g, cot_v[:, h * half:(h + 1) * half], deg[...])
-        for d in range(1, ng):
-            if h == 0:
+        if h == 0:
+            for d in range(1, ng):
                 deg_copy(d).wait_recv()
-            cot_copy(h, d).wait_recv()
-            scale(h, lax.rem(g - d + ng, ng), cot_in[h][d - 1], deg_in[d - 1])
-
-        def send_part(d, carry, h=h):
-            part_out[h][d - 1] = partial(h, lax.rem(b + d, nb)).astype(BF16)
-            part_copy(h, d).start()
+
+        def arrived(owner, h=h):
+            scale(h, owner, cot_in[h][owner], deg_in[lax.rem(g - owner + ng, ng) - 1])
+
+        for d in range(2, ng, 2):
+            cot_arrival(h, lax.rem(g - d + ng, ng)).wait_recv()
+            fwd_copy(h, d).start()
+        cot_arrival(h, sib).wait_recv()
+        arrived(sib)
+        for d in range(2, ng, 2):
+            arrived(lax.rem(g - d + ng, ng))
+        for d in range(2, ng, 2):
+            owner = lax.rem(sib - d + ng, ng)
+            cot_arrival(h, owner).wait_recv()
+            arrived(owner)
+
+        def send_part(i, carry, h=h):
+            d = lax.rem(i + nb - 2, nb - 1) + 1
+            d = d * (1 - 2 * upper) + nb * upper
+            value = partial(h, lax.rem(b + d, nb))
+            if not relay:
+                part_out[h][d - 1] = value.astype(BF16)
+                part_copy(h, d).start()
+                return carry
+            far = jnp.logical_and(at_end, i == 0)
+            join = jnp.logical_and(next_to_end, i == nb - 2)
+
+            @pl.when(join)
+            def _():
+                relay_copy(h, d).wait_recv()
+                part_out[h][d - 1] = (value + relay_in[h].astype(F32)).astype(BF16)
+
+            @pl.when(jnp.logical_not(join))
+            def _():
+                part_out[h][d - 1] = value.astype(BF16)
+
+            @pl.when(far)
+            def _():
+                relay_copy(h, d).start()
+
+            @pl.when(jnp.logical_not(far))
+            def _():
+                part_copy(h, d).start()
+
             return carry
 
-        lax.fori_loop(1, nb, send_part, 0)
+        if h == 1:
+            @pl.when(g < owners)
+            def _():
+                total = wq[pl.ds(pl.multiple_of(lax.rem(g, owners) * pr, pr), pr), :]
+                for d in range(1, ng):
+                    wg_copy(d)[1].wait_recv()
+                    total = total + wg_in[d - 1]
+                zag[b] = (total * factor).astype(BF16)
+                for d in range(1, nb):
+                    zag_copy(d).start()
+
+        lax.fori_loop(0, nb - 1, send_part, 0)
         acc[h][...] = partial(h, b)
 
         if h == 0:
@@ -165,43 +238,33 @@
                 to, copy = wg_copy(d)
                 pl.when(to < owners)(copy.start)
 
-    factor = (rows * nb * ng) ** (-0.5)
+    def write(q, first, values):
+        w_sum[pl.ds(pl.multiple_of(q * rq + first, pr), pr), :] = values
+
+    def finish(h):
+        for d in range(1, nb):
+            def add(d=d):
+                part_copy(h, d).wait_recv()
+                acc[h][...] += part_in[h][d - 1].astype(F32)
+
+            if relay and d == 1:
+                pl.when(b != 0)(add)
+            elif relay and d == nb - 1:
+                pl.when(b != nb - 1)(add)
+            else:
+                add()
+        pulled_b[:, h * half:(h + 1) * half] = acc[h][...].astype(BF16)
 
     @pl.when(g < owners)
     def _():
-        total = wq[pl.ds(pl.multiple_of(lax.rem(g, owners) * pr, pr), pr), :]
-        for d in range(1, ng):
-            wg_copy(d)[1].wait_recv()
-            total = total + wg_in[d - 1]
-        zag[b] = (total * factor).astype(BF16)
-        for d in range(1, nb):
-            zag_copy(d).start()
         for d in range(1, nb):
             zag_copy(d).wait_recv()
         for d in range(1, ng):
             gag_copy(d).start()
-
-    pulled = []
-    for h in range(HALVES):
-        total = acc[h][...]
-        for d in range(1, nb):
-            part_copy(h, d).wait_recv()
-            total = total + part_in[h][d - 1].astype(F32)
-        pulled.append(total.astype(BF16))
-    neigh = lax.dot_general(jnp.concatenate(pulled, axis=1), wn_v[...], dims1, preferred_element_type=F32)
-    gin[...] = (own[...] + neigh).astype(BF16)
-
-    def write(q, first, values):
-        per = width // rq
-        for out, base in ((gself, 0), (gneigh, per)):
-            if q // per * per == base:
-                out[pl.ds(pl.multiple_of((q - base) * rq + first, pr), pr), :] = values.astype(F32)
-
-    @pl.when(g < owners)
-    def _():
         for q in range(nb):
             write(q, lax.rem(g, owners) * pr, zag[q])
 
+    finish(0)
     for d in range(1, ng):
         owner = lax.rem(g - d + ng, ng)
 
@@ -211,18 +274,33 @@
             for q in range(nb):
                 write(q, lax.rem(owner, owners) * pr, gag[d - 1, q])
 
+    finish(1)
+
     for d in range(1, ng):
         deg_copy(d).wait_send()
-        for h in range(HALVES):
-            cot_copy(h, d).wait_send()
         to, copy = wg_copy(d)
         pl.when(to < owners)(copy.wait_send)
         pl.when(g < owners)(gag_copy(d).wait_send)
+    for h in range(HALVES):
+        cot_copy(h, 0).wait_send()
+        for d in range(2, ng, 2):
+            cot_copy(h, d).wait_send()
+            fwd_copy(h, d).wait_send()
     for d in range(1, nb):
         wz_copy(d).wait_send()
         for h in range(HALVES):
             part_copy(h, d).wait_send()
         pl.when(g < owners)(zag_copy(d).wait_send)
+
+
+def outputs(pulled_b, w_sum, cot, w_self, w_neigh, gin, gself, gneigh):
+    dims = (((1,), (1,)), ((), ()))
+    width = cot.shape[1]
+    own = lax.dot_general(cot[...], w_self[...], dims, preferred_element_type=F32)
+    neigh = lax.dot_general(pulled_b[...], w_neigh[...], dims, preferred_element_type=F32)
+    gin[...] = (own + neigh).astype(BF16)
+    gself[...] = w_sum[:width, :].astype(F32)
+    gneigh[...] = w_sum[width:, :].astype(F32)
 
 
 def on_device(nb, ng, node_feats, mean_feats, cotangent, w_self, w_neigh, degree, adjacency, dst_tiles, src_tiles, tile_counts):
@@ -238,40 +316,50 @@
     vmem, smem = pl.BlockSpec(memory_space=pltpu.VMEM), pl.BlockSpec(memory_space=pltpu.SMEM)
     dma = pltpu.SemaphoreType.DMA
     V = pltpu.VMEM
-    return pl.pallas_call(
+    pulled_b, w_sum = pl.pallas_call(
         functools.partial(kernel, dims),
         out_shape=(
             jax.ShapeDtypeStruct((rows, width), BF16),
-            jax.ShapeDtypeStruct((width, width), F32),
-            jax.ShapeDtypeStruct((width, width), F32),
+            jax.ShapeDtypeStruct((2 * width, width), BF16),
         ),
-        in_specs=[any_spec] * 5 + [vmem, any_spec] + [smem] * 3,
-        out_specs=(vmem, vmem, vmem),
+        in_specs=[any_spec] * 3 + [vmem, any_spec] + [smem] * 3,
+        out_specs=(vmem, vmem),
         scratch_shapes=[
             V((rows, width), BF16), V((rows, width), BF16), V((rows, width), BF16),
-            V((width, width), BF16), V((width, width), BF16), V(adjacency.shape, BF16),
-            V((ng - 1, rows, half), BF16), V((ng - 1, rows, half), BF16),
+            V(adjacency.shape, BF16),
+            V((ng, rows, half), BF16), V((ng, rows, half), BF16),
             V((ng - 1, dev_tiles, tile), jnp.int32),
             V((ng * dev_tiles, tile, width), BF16), V((ng * dev_tiles, tile, width), BF16),
             V((nb, rows, slots * tile), BF16),
             V((nb - 1, rows, half), BF16), V((nb - 1, rows, half), BF16),
             V((nb - 1, rows, half), BF16), V((nb - 1, rows, half), BF16),
-            V((rows, half), F32), V((rows, half), F32), V((rows, width), F32),
+            V((rows, half), F32), V((rows, half), F32), V((HALVES, rows, half), BF16),
             V((2 * width, width), F32), V((2 * width, width), BF16), V((nb - 1, rq, width), BF16),
             V((rq, width), F32), V((ng - 1, pr, width), F32),
             V((nb, pr, width), BF16), V((ng - 1, nb, pr, width), BF16),
-            dma((6,)),
-            dma((HALVES, ng - 1)), dma((HALVES, ng - 1)), dma((ng - 1,)), dma((ng - 1,)),
-            dma((HALVES, nb - 1)), dma((HALVES, nb - 1)), dma((nb - 1,)), dma((nb - 1,)),
+            dma((4,)),
+            dma((HALVES, 2, ng // 2)), dma((HALVES, ng)), dma((ng - 1,)), dma((ng - 1,)),
+            dma((HALVES, nb - 1)), dma((HALVES, nb - 1)), dma((HALVES,)), dma((nb - 1,)), dma((nb - 1,)),
             dma((ng - 1,)), dma((ng - 1,)), dma((nb - 1,)), dma((nb - 1,)), dma((ng - 1,)), dma((ng - 1,)),
         ],
         compiler_params=pltpu.CompilerParams(
             collective_id=0, has_side_effects=True, vmem_limit_bytes=56 * 1024 * 1024
         ),
     )(
-        cotangent, node_feats, mean_feats, w_self, w_neigh, degree.reshape(dev_tiles, tile),
+        cotangent, node_feats, mean_feats, degree.reshape(dev_tiles, tile),
         adjacency, dst_tiles, src_tiles, tile_counts,
     )
+    return pl.pallas_call(
+        outputs,
+        out_shape=(
+            jax.ShapeDtypeStruct((rows, width), BF16),
+            jax.ShapeDtypeStruct((width, width), F32),
+            jax.ShapeDtypeStruct((width, width), F32),
+        ),
+        in_specs=[vmem] * 5,
+        out_specs=(vmem, vmem, vmem),
+        compiler_params=pltpu.CompilerParams(vmem_limit_bytes=16 * 1024 * 1024),
+    )(pulled_b, w_sum, cotangent, w_self, w_neigh)
 
 
 def solution(mesh):

time: 48.1 us -> 40.2 us (0.84); the launches traced: 47.2 us -> 40 us
  Pallas kernels: 43.1 us -> 37.4 us
  local copies, waits for them, and re-layouts: 3.46 us -> 1.91 us
    pallas_call x1, Pallas kernels: 43.1 us -> 36.2 us  [on_device(): pl.pallas_call(functools.partial(kernel, dims), out_shape=(jax.ShapeDtype...]
    unnamed x7 -> x10, local copies, waits for them, and re-layouts: 3.46 us -> 1.91 us
    pallas_call x0 -> x1, Pallas kernels: none -> 1.15 us  [on_device(): pl.pallas_call(outputs, out_shape=(jax.ShapeDtypeStruct((rows, width), BF...]
where the time goes in v2:
time: 40.2 us; the launch traced here: 40 us
  Pallas kernels  37.4 us (93%)
  local copies, waits for them, and re-layouts  1.91 us (5%)
  between operations  0.7 us (2%)
    pallas_call x1, Pallas kernels, on_device(): pl.pallas_call(functools.partial(kernel, dims), out_shape=(jax.ShapeDtype...  36.2 us
    unnamed x10, local copies, waits for them, and re-layouts  1.91 us
    pallas_call x1, Pallas kernels, on_device(): pl.pallas_call(outputs, out_shape=(jax.ShapeDtypeStruct((rows, width), BF...  1.15 us

profile of v2, /device:TPU:0, one launch (start us, length us, event | category | flops | bytes accessed | tf_op | source)
XLA Modules:
  0.0 40.0 jit_solution(10218443489072652780)
XLA Ops:
  0.6 0.0 copy-start
  0.6 0.0 copy-start.3
  0.7 0.0 copy-start.4
  0.7 36.2 %shard_map.121 = (bf16[512,256]{1,0:T(8,128)(2,1)}, bf16[512,256]{1,0:T(8,128)(2,1)}) custom-call(bf16[512,256]{1,0:T(8,128)(2,1)} %cot.3, bf16[512,256]{1,0:T(8,128)(2,1)} %node.1, bf16[512,256]{1,0:T(8,128)(2,1)} %mean.1, s32[4,128]{1,0:T(4,128)} %bitcast.1, bf16[1,1,4,6,128,128]{5,4,3,2,1,0:T(8,128)(2,1)} %adj.1, s32[1,1,4,6]{3,2,1,0:T(4,128)} %dst.1, ...), custom_call_target="tpu_custom_call" | custom-call | tf_op jit(solution)/shard_map/pallas_call | solution.py:319
  36.9 0.0 copy-done
  36.9 0.0 copy-done.3
  36.9 0.0 copy-done.4
  36.9 0.0 copy-start.1
  36.9 0.9 %copy-done.1 = bf16[512,256]{1,0:T(8,128)(2,1)S(1)} copy-done((bf16[512,256]{1,0:T(8,128)(2,1)S(1)}, bf16[512,256]{1,0:T(8,128)(2,1)}, u32[]{:S(2)}) %copy-start.1) | copy-done | bytes 262168
  37.9 0.0 copy-start.2
  37.9 0.9 %copy-done.2 = bf16[512,256]{1,0:T(8,128)(2,1)S(1)} copy-done((bf16[512,256]{1,0:T(8,128)(2,1)S(1)}, bf16[512,256]{1,0:T(8,128)(2,1)}, u32[]{:S(2)}) %copy-start.2) | copy-done | bytes 262168
  38.8 1.2 %shard_map.122 = (bf16[512,256]{1,0:T(8,128)(2,1)}, f32[256,256]{1,0:T(8,128)}, f32[256,256]{1,0:T(8,128)}) custom-call(bf16[512,256]{1,0:T(8,128)(2,1)S(1)} %copy-done.1, bf16[512,256]{1,0:T(8,128)(2,1)S(1)} %copy-done.2, bf16[512,256]{1,0:T(8,128)(2,1)S(1)} %copy-done, bf16[256,256]{1,0:T(8,128)(2,1)S(1)} %copy-done.3, bf16[256,256]{1,0:T(8,128)(2,1)S(1)} %copy-done.4), custom_call_target="tpu_custom_call" | custom-call | tf_op jit(solution)/shard_map/pallas_call | solution.py:352
Async XLA Ops:
  0.6 36.3 %copy-start = (bf16[512,256]{1,0:T(8,128)(2,1)S(1)}, bf16[512,256]{1,0:T(8,128)(2,1)}, u32[]{:S(2)}) copy-start(bf16[512,256]{1,0:T(8,128)(2,1)} %cot.3) | copy-start | bytes 786436
  0.6 36.3 %copy-start.3 = (bf16[256,256]{1,0:T(8,128)(2,1)S(1)}, bf16[256,256]{1,0:T(8,128)(2,1)}, u32[]{:S(2)}) copy-start(bf16[256,256]{1,0:T(8,128)(2,1)} %w_self.1) | copy-start | bytes 393220
  0.7 36.3 %copy-start.4 = (bf16[256,256]{1,0:T(8,128)(2,1)S(1)}, bf16[256,256]{1,0:T(8,128)(2,1)}, u32[]{:S(2)}) copy-start(bf16[256,256]{1,0:T(8,128)(2,1)} %w_neigh.1) | copy-start | bytes 393220
  36.9 1.0 %copy-start.1 = (bf16[512,256]{1,0:T(8,128)(2,1)S(1)}, bf16[512,256]{1,0:T(8,128)(2,1)}, u32[]{:S(2)}) copy-start(bf16[512,256]{1,0:T(8,128)(2,1)} %get-tuple-element.5.pulled_b) | copy-start | bytes 786436
  37.9 0.9 %copy-start.2 = (bf16[512,256]{1,0:T(8,128)(2,1)S(1)}, bf16[512,256]{1,0:T(8,128)(2,1)}, u32[]{:S(2)}) copy-start(bf16[512,256]{1,0:T(8,128)(2,1)} %get-tuple-element.6.w_sum) | copy-start | bytes 786436

commit v3 on v2

--- a/solution.py
+++ b/solution.py
@@ -18,7 +18,7 @@
     pulled_b, w_sum,
     cot_v, node_v, mean_v, adj_v,
     cot_in0, cot_in1, deg_in, scaled0, scaled1, placed,
-    part_out0, part_out1, part_in0, part_in1, acc0, acc1, relay_in,
+    part_out0, part_out1, part_in0, part_in1, acc0, acc1, relay_in, held,
     w_acc, w_out, wz_in, wq, wg_in, zag, gag,
     load_sem, gs, gr, ds, dr, ps, pr_sem, rr, zs, zr, qs, qr, as_, ar, bs, br,
 ):
@@ -55,7 +55,7 @@
     def cot_copy(h, d):
         to = sib if d == 0 else lax.rem(g + d, ng)
         return pltpu.make_async_remote_copy(
-            src_ref=cot.at[:, pl.ds(h * half, half)], dst_ref=cot_in[h].at[g],
+            src_ref=cot_v.at[:, pl.ds(h * half, half)], dst_ref=cot_in[h].at[g],
             send_sem=gs.at[h, 0, d // 2], recv_sem=gr.at[h, g],
             device_id={"grp": to}, device_id_type=MESH)
 
@@ -72,14 +72,14 @@
             send_sem=gs.at[h, 0, 0], recv_sem=gr.at[h, owner],
             device_id={"grp": sib}, device_id_type=MESH)
 
+    loads[0].wait()
     for d in range(1, ng):
         deg_copy(d).start()
-    for h in range(HALVES):
-        for d in range(2, ng, 2):
-            cot_copy(h, d).start()
-        cot_copy(h, 0).start()
-
-    for c in loads[:3]:
+    for d in range(2, ng, 2):
+        cot_copy(0, d).start()
+    cot_copy(0, 0).start()
+
+    for c in loads[1:3]:
         c.wait()
     dims0 = (((0,), (0,)), ((), ()))
     for i, feats in enumerate((node_v, mean_v)):
@@ -163,6 +163,12 @@
     upper = b // (nb // 2)
     factor = (rows * nb * ng) ** (-0.5)
 
+    def join_far(h):
+        d = (nb - 2) * (1 - upper) + 2 * upper
+        relay_copy(h, d).wait_recv()
+        part_out[h][d - 1] = (held[h] + relay_in[h].astype(F32)).astype(BF16)
+        part_copy(h, d).start()
+
     for h in range(HALVES):
         scale(h, g, cot_v[:, h * half:(h + 1) * half], deg[...])
         if h == 0:
@@ -175,6 +181,10 @@
         for d in range(2, ng, 2):
             cot_arrival(h, lax.rem(g - d + ng, ng)).wait_recv()
             fwd_copy(h, d).start()
+        if h + 1 < HALVES:
+            for d in range(2, ng, 2):
+                cot_copy(h + 1, d).start()
+            cot_copy(h + 1, 0).start()
         cot_arrival(h, sib).wait_recv()
         arrived(sib)
         for d in range(2, ng, 2):
@@ -197,8 +207,7 @@
 
             @pl.when(join)
             def _():
-                relay_copy(h, d).wait_recv()
-                part_out[h][d - 1] = (value + relay_in[h].astype(F32)).astype(BF16)
+                held[h] = value
 
             @pl.when(jnp.logical_not(join))
             def _():
@@ -208,7 +217,7 @@
             def _():
                 relay_copy(h, d).start()
 
-            @pl.when(jnp.logical_not(far))
+            @pl.when(jnp.logical_not(jnp.logical_or(far, join)))
             def _():
                 part_copy(h, d).start()
 
@@ -225,6 +234,8 @@
                 for d in range(1, nb):
                     zag_copy(d).start()
 
+        if relay and h == 1:
+            pl.when(next_to_end)(functools.partial(join_far, 0))
         lax.fori_loop(0, nb - 1, send_part, 0)
         acc[h][...] = partial(h, b)
 
@@ -237,6 +248,9 @@
             for d in range(1, ng):
                 to, copy = wg_copy(d)
                 pl.when(to < owners)(copy.start)
+
+    if relay:
+        pl.when(next_to_end)(functools.partial(join_far, 1))
 
     def write(q, first, values):
         w_sum[pl.ds(pl.multiple_of(q * rq + first, pr), pr), :] = values
@@ -333,7 +347,7 @@
             V((nb, rows, slots * tile), BF16),
             V((nb - 1, rows, half), BF16), V((nb - 1, rows, half), BF16),
             V((nb - 1, rows, half), BF16), V((nb - 1, rows, half), BF16),
-            V((rows, half), F32), V((rows, half), F32), V((HALVES, rows, half), BF16),
+            V((rows, half), F32), V((rows, half), F32), V((HALVES, rows, half), BF16), V((HALVES, rows, half), F32),
             V((2 * width, width), F32), V((2 * width, width), BF16), V((nb - 1, rq, width), BF16),
             V((rq, width), F32), V((ng - 1, pr, width), F32),
             V((nb, pr, width), BF16), V((ng - 1, nb, pr, width), BF16),
@@ -358,7 +372,7 @@
         ),
         in_specs=[vmem] * 5,
         out_specs=(vmem, vmem, vmem),
-        compiler_params=pltpu.CompilerParams(vmem_limit_bytes=16 * 1024 * 1024),
+        compiler_params=pltpu.CompilerParams(vmem_limit_bytes=56 * 1024 * 1024),
     )(pulled_b, w_sum, cotangent, w_self, w_neigh)
 
 

time: 40.2 us -> 38.5 us (0.958)
  local copies, waits for them, and re-layouts: 1.91 us -> 0 us
    unnamed x10 -> x0, local copies, waits for them, and re-layouts: 1.91 us -> none
    pallas_call x1, Pallas kernels: 1.15 us -> 2.35 us  [on_device(): pl.pallas_call(outputs, out_shape=(jax.ShapeDtypeStruct((rows, width), BF...]
    pallas_call x1, Pallas kernels: 36.2 us -> 35.4 us  [on_device(): pl.pallas_call(functools.partial(kernel, dims), out_shape=(jax.ShapeDtype...]
where the time goes in v3:
time: 38.5 us; the launch traced here: 38.4 us
  Pallas kernels  37.7 us (98%)
  between operations  0.64 us (2%)
    pallas_call x1, Pallas kernels, on_device(): pl.pallas_call(functools.partial(kernel, dims), out_shape=(jax.ShapeDtype...  35.4 us
    pallas_call x1, Pallas kernels, on_device(): pl.pallas_call(outputs, out_shape=(jax.ShapeDtypeStruct((rows, width), BF...  2.35 us

profile of v3, /device:TPU:0, one launch (start us, length us, event | category | flops | bytes accessed | tf_op | source)
XLA Modules:
  0.0 38.4 jit_solution(17383790362154722967)
XLA Ops:
  0.6 35.4 %shard_map.121 = (bf16[512,256]{1,0:T(8,128)(2,1)}, bf16[512,256]{1,0:T(8,128)(2,1)}) custom-call(bf16[512,256]{1,0:T(8,128)(2,1)} %cot.3, bf16[512,256]{1,0:T(8,128)(2,1)} %node.1, bf16[512,256]{1,0:T(8,128)(2,1)} %mean.1, s32[4,128]{1,0:T(4,128)} %bitcast.1, bf16[1,1,4,6,128,128]{5,4,3,2,1,0:T(8,128)(2,1)} %adj.1, s32[1,1,4,6]{3,2,1,0:T(4,128)} %dst.1, ...), custom_call_target="tpu_custom_call" | custom-call | tf_op jit(solution)/shard_map/pallas_call | solution.py:333
  36.0 2.4 %shard_map.122 = (bf16[512,256]{1,0:T(8,128)(2,1)}, f32[256,256]{1,0:T(8,128)}, f32[256,256]{1,0:T(8,128)}) custom-call(bf16[512,256]{1,0:T(8,128)(2,1)} %get-tuple-element.5.pulled_b, bf16[512,256]{1,0:T(8,128)(2,1)} %get-tuple-element.6.w_sum, bf16[512,256]{1,0:T(8,128)(2,1)} %cot.3, bf16[256,256]{1,0:T(8,128)(2,1)} %w_self.1, bf16[256,256]{1,0:T(8,128)(2,1)} %w_neigh.1), custom_call_target="tpu_custom_call" | custom-call | tf_op jit(solution)/shard_map/pallas_call | solution.py:366

commit v4 on v3

--- a/solution.py
+++ b/solution.py
@@ -307,14 +307,32 @@
         pl.when(g < owners)(zag_copy(d).wait_send)
 
 
-def outputs(pulled_b, w_sum, cot, w_self, w_neigh, gin, gself, gneigh):
+def outputs(pulled_b, w_sum, cot, w_self, w_neigh, gin, gself, gneigh, pv, wv, cv, sv, nv, gv, selfv, neighv, isem, osem):
     dims = (((1,), (1,)), ((), ()))
     width = cot.shape[1]
-    own = lax.dot_general(cot[...], w_self[...], dims, preferred_element_type=F32)
-    neigh = lax.dot_general(pulled_b[...], w_neigh[...], dims, preferred_element_type=F32)
-    gin[...] = (own + neigh).astype(BF16)
-    gself[...] = w_sum[:width, :].astype(F32)
-    gneigh[...] = w_sum[width:, :].astype(F32)
+    loads = [
+        pltpu.make_async_copy(x, v, isem.at[i])
+        for i, (x, v) in enumerate(((w_sum, wv), (cot, cv), (w_self, sv), (pulled_b, pv), (w_neigh, nv)))
+    ]
+    stores = [
+        pltpu.make_async_copy(v, x, osem.at[i])
+        for i, (v, x) in enumerate(((selfv, gself), (neighv, gneigh), (gv, gin)))
+    ]
+    for c in loads:
+        c.start()
+    loads[0].wait()
+    selfv[...] = wv[:width, :].astype(F32)
+    stores[0].start()
+    neighv[...] = wv[width:, :].astype(F32)
+    stores[1].start()
+    for c in loads[1:]:
+        c.wait()
+    own = lax.dot_general(cv[...], sv[...], dims, preferred_element_type=F32)
+    neigh = lax.dot_general(pv[...], nv[...], dims, preferred_element_type=F32)
+    gv[...] = (own + neigh).astype(BF16)
+    stores[2].start()
+    for c in stores:
+        c.wait()
 
 
 def on_device(nb, ng, node_feats, mean_feats, cotangent, w_self, w_neigh, degree, adjacency, dst_tiles, src_tiles, tile_counts):
@@ -370,8 +388,13 @@
             jax.ShapeDtypeStruct((width, width), F32),
             jax.ShapeDtypeStruct((width, width), F32),
         ),
-        in_specs=[vmem] * 5,
-        out_specs=(vmem, vmem, vmem),
+        in_specs=[any_spec] * 5,
+        out_specs=(any_spec, any_spec, any_spec),
+        scratch_shapes=[
+            V((rows, width), BF16), V((2 * width, width), BF16), V((rows, width), BF16),
+            V((width, width), BF16), V((width, width), BF16), V((rows, width), BF16),
+            V((width, width), F32), V((width, width), F32), dma((5,)), dma((3,)),
+        ],
         compiler_params=pltpu.CompilerParams(vmem_limit_bytes=56 * 1024 * 1024),
     )(pulled_b, w_sum, cotangent, w_self, w_neigh)
 

time: 38.5 us -> 38.5 us (level)
  no operation moved by 1% of the time
where the time goes in v4:
time: 38.5 us; the launch traced here: 38.3 us
  Pallas kernels  37.7 us (98%)
  between operations  0.64 us (2%)
    pallas_call x1, Pallas kernels, on_device(): pl.pallas_call(functools.partial(kernel, dims), out_shape=(jax.ShapeDtype...  35.4 us
    pallas_call x1, Pallas kernels, on_device(): pl.pallas_call(outputs, out_shape=(jax.ShapeDtypeStruct((rows, width), BF...  2.28 us

profile of v4, /device:TPU:0, one launch (start us, length us, event | category | flops | bytes accessed | tf_op | source)
XLA Modules:
  0.0 38.3 jit_solution(2404411173274177932)
XLA Ops:
  0.6 35.4 %shard_map.121 = (bf16[512,256]{1,0:T(8,128)(2,1)}, bf16[512,256]{1,0:T(8,128)(2,1)}) custom-call(bf16[512,256]{1,0:T(8,128)(2,1)} %cot.3, bf16[512,256]{1,0:T(8,128)(2,1)} %node.1, bf16[512,256]{1,0:T(8,128)(2,1)} %mean.1, s32[4,128]{1,0:T(4,128)} %bitcast.1, bf16[1,1,4,6,128,128]{5,4,3,2,1,0:T(8,128)(2,1)} %adj.1, s32[1,1,4,6]{3,2,1,0:T(4,128)} %dst.1, ...), custom_call_target="tpu_custom_call" | custom-call | tf_op jit(solution)/shard_map/pallas_call | solution.py:351
  36.0 2.3 %shard_map.122 = (bf16[512,256]{1,0:T(8,128)(2,1)}, f32[256,256]{1,0:T(8,128)}, f32[256,256]{1,0:T(8,128)}) custom-call(bf16[512,256]{1,0:T(8,128)(2,1)} %get-tuple-element.5.pulled_b, bf16[512,256]{1,0:T(8,128)(2,1)} %get-tuple-element.6.w_sum, bf16[512,256]{1,0:T(8,128)(2,1)} %cot.3, bf16[256,256]{1,0:T(8,128)(2,1)} %w_self.1, bf16[256,256]{1,0:T(8,128)(2,1)} %w_neigh.1), custom_call_target="tpu_custom_call" | custom-call | tf_op jit(solution)/shard_map/pallas_call | solution.py:384
